TPU v7x, 128 devices: a whole 4x4x4 slice. The times are simulated.
128 devices in a mesh: dp: 8 (over y, x_hi), fsdp: 16 (over z, x_lo, core).
Axes of the slice: x: 4 (x_hi: 2, x_lo: 2; x = x_hi * 2 + x_lo), y: 4, z: 4, core: 2. Of those that a mesh axis runs over, the one named last changes fastest.
Arguments:
- features: bfloat16 [65536, 6144], P(('dp', 'fsdp')), may hold values from -125 to 125
- head_weight: bfloat16 [6144, 512], P('fsdp'), may hold values from -0.21875 to 0.21875
- probe_seeds: int32 [2], replicated, may hold values from 0 to 999999
Outputs:
- hvp: float32 [6144, 2, 512], P('fsdp')
- rayleigh: float32 [2], replicated
All inputs are finite; a program needn't handle non-finite values.
Results may differ from a plain program's by a relative error of at most 0.015.
Values may be sent and summed in bfloat16 or wider, within the bound.
A program may use at most 128 MiB of HBM per device.

v0:
```python
import math

import jax
import jax.numpy as jnp
from jax import lax
from jax.sharding import PartitionSpec as P


def probe_signs(probe_seeds, row_count, class_count):
    row_ids = jnp.arange(row_count, dtype=jnp.int32)[:, None]
    col_ids = jnp.arange(class_count, dtype=jnp.int32)[None, :]
    flat_index = row_ids * class_count + col_ids
    signs_list = []
    for probe_id in range(2):
        mixing = flat_index ^ probe_seeds[probe_id] * 668265261
        mixing = mixing * 747796405 + 289555
        mixing = (mixing ^ mixing >> 15 & 131071) * 277803737
        mixing = mixing ^ mixing >> 16 & 65535
        signs_list.append(((mixing >> 7 & 1) * 2 - 1).astype(jnp.float32))
    return jnp.concatenate(signs_list, axis=1).astype(jnp.bfloat16)


def shards(features, head_weight, probe_seeds):
    groups = lax.axis_size("fsdp")
    data_count = lax.axis_size("dp")
    local_rows = head_weight.shape[0]
    class_count = head_weight.shape[1]
    image_count = features.shape[0]
    width_total = local_rows * groups
    all_images = image_count * groups * data_count
    loss_scale = 32.0 / math.sqrt(all_images * width_total)
    columns = features
    logits = jnp.dot(
        columns,
        lax.all_gather(head_weight, "fsdp", axis=0, tiled=True),
        preferred_element_type=jnp.float32,
    )
    whole_probes = probe_signs(probe_seeds, width_total, class_count)
    tangents = jnp.dot(features, whole_probes, preferred_element_type=jnp.float32)
    tangents = tangents.reshape(image_count, 2, class_count)
    chances = jax.nn.softmax(logits, axis=-1)[:, None, :]
    centre = jnp.sum(chances * tangents, axis=-1, keepdims=True)
    curved = loss_scale * chances * (tangents - centre)
    quotient = lax.psum(jnp.sum(tangents * curved, axis=(0, 2)), ("dp", "fsdp"))
    rounded = curved.reshape(image_count, 2 * class_count).astype(jnp.bfloat16)
    columns = features
    group_sum = lax.psum_scatter(
        lax.dot_general(
            columns, rounded, (((0,), (0,)), ((), ())), preferred_element_type=jnp.float32
        ),
        "fsdp",
        scatter_dimension=0,
        tiled=True,
    )
    hvp_rows = lax.psum(group_sum, "dp")
    hvp_rows = hvp_rows.reshape(local_rows, 2, class_count)
    return (hvp_rows, quotient / (width_total * class_count))


def solution(mesh):
    return jax.shard_map(
        shards,
        mesh=mesh,
        in_specs=(P(("dp", "fsdp"), None), P("fsdp", None), P()),
        out_specs=(P("fsdp", None, None), P()),
        check_vma=False,
    )
```

profile of v0, /device:TPU:0, one launch (start us, length us, event | category | flops | bytes accessed | tf_op | source)
XLA Modules:
  0.0 455.6 jit_solution(13546888605349900812)
XLA Ops:
  7.2 0.0 all-gather.2.cloned.1.call-start
  7.2 0.7 all-gather.2.cloned.1.call-update
  7.9 0.0 reduce-scatter.2.cloned.1.call-start
  7.9 1.3 fusion.14
  10.6 15.3 %convert_convert_fusion.1 = (bf16[6144,512]{1,0:T(8,128)(2,1)}, bf16[6144,512]{1,0:T(8,128)(2,1)}) fusion(s32[]{:T(128)} %bitcast.1, s32[6144]{0:T(1024)S(1)} %iota_multiply_fusion, s32[]{:T(128)} %bitcast.2), kind=kLoop, calls=%fused_computation.7 | loop fusion | flops 103809024 | bytes 12607496 | tf_op jit(solution)/shard_map/convert
  25.9 11.8 %fusion.1 = f32[1024,512]{1,0:T(8,128)S(1)} fusion(bf16[512,6144]{1,0:T(8,128)(2,1)} %param.3, bf16[6144,512]{1,0:T(8,128)(2,1)} %get-tuple-element.7, bf16[6144,512]{1,0:T(8,128)(2,1)} %get-tuple-element.6), kind=kOutput, calls=%fused_computation.2 | convolution fusion | flops 6467616768 | bytes 20971520 | tf_op jit(solution)/shard_map/dot_general | solution.py:39
  37.7 16.9 %all-gather.2.cloned.1.call-done = bf16[6144,512]{1,0:T(8,128)(2,1)} async-done(((bf16[384,512]{1,0:T(8,128)(2,1)}), bf16[6144,512]{1,0:T(8,128)(2,1)}) %all-gather.2.cloned.1.call-update) | async-done | bytes 6291472 | tf_op jit(solution)/shard_map/all_gather | solution.py:35
  54.6 8.5 %fusion.15 = (f32[512]{0:T(512)S(1)}, f32[512,512]{0,1:T(8,128)S(1)}) fusion(bf16[512,6144]{1,0:T(8,128)(2,1)} %param.3, bf16[6144,512]{1,0:T(8,128)(2,1)} %all-gather.2.cloned.1.call-done), kind=kOutput, calls=%fused_computation.25 | convolution fusion | flops 3221487104 | bytes 13633536 | tf_op jit(solution)/shard_map/dot_general | solution.py:33
  63.1 0.0 slice-start
  63.1 0.2 fusion.11
  63.3 0.2 broadcast_multiply_fusion
  63.5 0.0 slice-start.1
  63.5 0.8 fusion
  64.3 0.4 fusion.6
  64.8 0.0 slice-done
  64.8 1.2 slice-done.1
  66.0 11.8 %convolution_bitcast_fusion = f32[6144,1024]{0,1:T(8,128)} fusion(bf16[512,1024]{0,1:T(8,128)(2,1)S(1)} %get-tuple-element.5, bf16[512,6144]{1,0:T(8,128)(2,1)S(1)} %bitcast.39), kind=kOutput, calls=%fused_computation.1 | convolution fusion | flops 6442450944 | bytes 32505856 | tf_op jit(solution)/shard_map/dot_general | solution.py:48
  77.8 0.0 reduce-scatter.2.cloned.1.call-update
  77.8 0.0 all-reduce.2.cloned.1.call-start
  77.9 268.0 %reduce-scatter.2.cloned.1.call-done = f32[384,1024]{0,1:T(8,128)} async-done(((f32[6144,1024]{0,1:T(8,128)}), f32[384,1024]{0,1:T(8,128)}) %reduce-scatter.2.cloned.1.call-update) | async-done | bytes 1572880 | tf_op jit(solution)/shard_map/reduce_scatter | solution.py:47
  345.9 3.7 copy.6
  349.6 0.0 all-reduce.2.cloned.1.call-update
  349.6 0.1 reduce_sum.38
  349.7 77.4 %psum.15 = f32[2]{0:T(128)S(1)} all-reduce(f32[2]{0:T(128)S(1)} %reduce_sum.38), channel_id=1, replica_groups=mesh['dp'=8,'fsdp'=16] {'dp','fsdp'}, use_global_device_ids=true, to_apply=%region_7.8 | all-reduce | flops 2 | bytes 16 | tf_op jit(solution)/shard_map/psum | solution.py:44
  427.1 0.5 broadcast_multiply_fusion.1
  427.7 18.3 %all-reduce.2.cloned.1.call-done = f32[384,2,512]{2,1,0:T(2,128)} async-done(((f32[384,2,512]{2,1,0:T(2,128)}), f32[384,2,512]{2,1,0:T(2,128)}) %all-reduce.2.cloned.1.call-update) | async-done | bytes 1572880 | tf_op jit(solution)/shard_map/psum | solution.py:55
  446.0 3.1 copy.8
  (3 shorter events, 0.0 us)
Async XLA Ops:
  7.2 47.4 %all-gather.2.cloned.1.call-start = ((), (), s32[]{:S(2)}) async-start(), calls=%async_computation.1 | async-start | bytes 6684672 | tf_op jit(solution)/shard_map/all_gather | solution.py:35
  7.9 338.0 %reduce-scatter.2.cloned.1.call-start = ((), (), s32[]{:S(2)}) async-start(), calls=%async_computation.2 | async-start | bytes 26738688 | tf_op jit(solution)/shard_map/reduce_scatter | solution.py:47
  63.1 1.7 slice-start
  63.5 2.5 slice-start.1
  77.8 368.2 %all-reduce.2.cloned.1.call-start = ((), (), s32[]{:S(2)}) async-start(), calls=%async_computation.3 | async-start | bytes 3145728 | tf_op jit(solution)/shard_map/psum | solution.py:55
Sparse Core Ops, SparseCore 0:
  9.7 44.8 all-gather.1
  77.9 267.9 reduce-scatter.1
  349.7 96.2 all-reduce.1
where the time goes:
time: 456 us
  waiting for transfers between devices  304 us (67%)
  blocking collectives  77.4 us (17%)
  matrix products  32 us (7%)
  other arithmetic  17.6 us (4%)
  between operations  15.1 us (3%)
  local copies, waits for them, and re-layouts  9.32 us (2%)
    reduce_scatter x1, waiting for transfers between devices, shards(): lax.psum_scatter(lax.dot_general(columns, rounded, (((0,), (0,)), ((), ()...  268 us
    psum x1, blocking collectives, shards(): quotient = lax.psum(jnp.sum(tangents * curved, axis=(0, 2)), ('dp', 'fsdp'))  77.4 us
    psum x1, waiting for transfers between devices, shards(): hvp_rows = lax.psum(group_sum, 'dp')  18.3 us
    all_gather x1, waiting for transfers between devices, shards(): lax.all_gather(head_weight, 'fsdp', axis=0, tiled=True)  16.9 us
    another operation x1, other arithmetic  15.3 us
    dot_general x1, matrix products, shards(): jnp.dot(features, whole_probes, preferred_element_type=jnp.float32)  11.8 us
    dot_general x1, matrix products, shards(): lax.dot_general(columns, rounded, (((0,), (0,)), ((), ())), preferred_ele...  11.8 us
  transfers between devices with their start and end apart: 3, of which 3 were waited for; matrix products, arithmetic and copies ran while one was open for 6% of the time, Pallas kernels for 0%

commit v1 on v0

v1 whole, which is shorter than its diff:
```python
import functools
import math

import jax
import jax.numpy as jnp
from jax import lax
from jax.experimental import pallas as pl
from jax.experimental.pallas import tpu as pltpu
from jax.sharding import PartitionSpec as P

MESH = pl.DeviceIdType.MESH
F32, BF16, I32 = jnp.float32, jnp.bfloat16, jnp.int32
CLS = 512
ROWS = 384
IMG = 512
PAIR = 2 * ROWS
HALF_D = 8 * ROWS
ORDERS = (("z", "x", "y"), ("x", "z", "y"), ("y", "z", "x"))
WRAP_MUL = ((277803737 << 8) + (1 << 31)) % (1 << 32) - (1 << 31)


def place():
    dp, fs = lax.axis_index("dp"), lax.axis_index("fsdp")
    return {"x": (dp % 2) * 2 + (fs // 2) % 2, "y": dp // 2, "z": fs // 4, "c": fs % 2}


def device(at, **offsets):
    x = (at["x"] + offsets.get("x", 0) + 4) % 4
    y = (at["y"] + offsets.get("y", 0) + 4) % 4
    z = (at["z"] + offsets.get("z", 0) + 4) % 4
    c = (at["c"] + offsets.get("c", 0)) % 2
    return {"dp": y * 2 + x // 2, "fsdp": (z * 2 + x % 2) * 2 + c}


def contract_last(a, b):
    return lax.dot_general(a, b, (((1,), (1,)), ((), ())), preferred_element_type=F32)


def kernel(
    loss_scale, inv_count, feat, head, seeds, out, quot,
    f, st, wt, tan, tan_in, log, log_in, ct, prod, r1, r2, r3, fin, q_mine, q_in,
    load_sem, send_sem, recv_sem,
):
    at = place()
    x, y, z, c = at["x"], at["y"], at["z"], at["c"]
    xl, xh = x % 2, x // 2
    peer = device(at, c=1)
    ids = {}
    started = []

    def copy(name, src, dst, to):
        if name not in ids:
            ids[name] = len(ids)
        i = ids[name]
        return pltpu.make_async_remote_copy(
            src_ref=src, dst_ref=dst, send_sem=send_sem.at[i], recv_sem=recv_sem.at[i],
            device_id=to, device_id_type=MESH,
        )

    flying = {}

    def send(name, src, dst, to):
        one = copy(name, src, dst, to)
        one.start()
        flying[name] = one
        started.append(one)

    def recv(name):
        flying[name].wait_recv()

    barrier = pltpu.get_barrier_semaphore()
    partners = [peer]
    for axis in "xyz":
        partners += [device(at, **{axis: s}) for s in (1, 2, 3)]
    partners += [device(at, x=2, y=s) for s in (1, 2, 3)]
    for to in partners:
        pl.semaphore_signal(barrier, inc=1, device_id=to, device_id_type=MESH)

    loads = []
    for b in range(8):
        col = pl.multiple_of((2 * b + c) * ROWS, 128)
        one = pltpu.make_async_copy(
            feat.at[:, pl.ds(col, ROWS)], f.at[pl.ds(0, IMG), pl.ds(b * ROWS, ROWS)], load_sem.at[b]
        )
        one.start()
        loads.append(one)

    own_cols = pl.ds(pl.multiple_of(xl * ROWS, 128), ROWS)
    wt[0, :, own_cols] = head[...].T

    pl.semaphore_wait(barrier, len(partners))

    top, bottom = pl.ds(0, CLS // 2), pl.ds(CLS // 2, CLS // 2)
    halves = (("a", top, 1), ("b", bottom, -1))
    for h, rows, way in halves:
        own = wt.at[0, rows, own_cols]
        send(f"wx0{h}", own, own, device(at, x=way))
        for s in (1, 3, 2):
            send(f"wz{s}{h}", own, wt.at[4 - s, rows, own_cols], device(at, z=s))
    for b in range(8):
        col = pl.multiple_of((2 * b + 1 - c) * ROWS, 128)
        send(f"f{b}", feat.at[:, pl.ds(col, ROWS)], f.at[pl.ds(IMG, IMG), pl.ds(b * ROWS, ROWS)], peer)

    def forward(s, h, rows, way):
        recv(f"wz{s}{h}")
        block = wt.at[4 - s, rows, own_cols]
        send(f"wx{4 - s}{h}", block, block, device(at, x=way))

    for k in range(2):
        key = seeds[k] * 668265261
        low, high = key & 511, key & ~511
        for b in range(8):
            @pl.loop(0, CLS // 16)
            def _(r):
                d = lax.broadcasted_iota(I32, (16, ROWS), 1) + (2 * b + c) * ROWS
                rows_mixed = ((d * CLS) ^ high) * 747796405 + 289555
                cls = lax.broadcasted_iota(I32, (16, ROWS), 0) + r * 16
                h = rows_mixed + (cls ^ low) * 747796405
                h = (h ^ lax.shift_right_logical(h, 15)) * WRAP_MUL
                h = h ^ (h << 16)
                st[pl.ds(pl.multiple_of(k * CLS + r * 16, 16), 16), b * ROWS:(b + 1) * ROWS] = jnp.where(
                    h < 0, 1.0, -1.0).astype(BF16)

    def tangents(side, tile):
        rows = slice(side * IMG + tile * 256, side * IMG + (tile + 1) * 256)
        tan[side, :, tile * 256:(tile + 1) * 256] = contract_last(st[...], f[rows, :])

    for one in loads:
        one.wait()
    tangents(0, 0)
    for s in (1, 3):
        forward(s, *halves[0])
    tangents(0, 1)
    for b in range(8):
        recv(f"f{b}")
    tangents(1, 0)
    for s in (1, 3):
        forward(s, *halves[1])
    tangents(1, 1)
    send("tan", tan.at[1], tan_in, peer)

    def logits(rz, side):
        col = pl.multiple_of(((z + rz) % 4) * PAIR, 128)
        part = contract_last(wt[rz], f[side * IMG:(side + 1) * IMG, pl.ds(col, PAIR)])
        if rz == 0:
            log[side] = part
        else:
            log[side] += part

    for h in "ab":
        recv(f"wx0{h}")
    for side in (1, 0):
        logits(0, side)
    for half in halves:
        forward(2, *half)
    for rz in (3, 1, 2):
        for h in "ab":
            recv(f"wx{rz}{h}")
        logits(rz, 1)
        if rz == 2:
            send("log", log.at[1], log_in, peer)
        logits(rz, 0)
    recv("tan")
    recv("log")

    for t in range(4):
        cols = slice(t * 128, (t + 1) * 128)
        total = log[0, :, cols] + log_in[:, cols]
        e = jnp.exp(total - jnp.max(total, axis=0, keepdims=True))
        log[0, :, cols] = e * (1.0 / jnp.sum(e, axis=0, keepdims=True))
    q_mine[...] = jnp.zeros_like(q_mine)
    for k in range(2):
        for t in range(4):
            cols = slice(t * 128, (t + 1) * 128)
            rows = slice(k * CLS, (k + 1) * CLS)
            chances = log[0, :, cols]
            tangent = tan[0, rows, cols] + tan_in[rows, cols]
            centre = jnp.sum(chances * tangent, axis=0, keepdims=True)
            curved = loss_scale * chances * (tangent - centre)
            q_mine[k:k + 1, :] += jnp.sum(tangent * curved, axis=0, keepdims=True)
            ct[rows, cols] = curved.astype(BF16)
        half = ct.at[pl.ds(k * CLS, CLS), pl.ds(0, IMG)]
        send(f"ct{k}", half, ct.at[pl.ds(k * CLS, CLS), pl.ds(IMG, IMG)], peer)

    send("qc", q_mine, q_in.at[0, 0], peer)

    def q_stage(stage, axis):
        if stage == 1:
            recv("qc")
            mine = q_mine[...] + q_in[0, 0]
        else:
            for s in (1, 2, 3):
                recv(f"q{stage - 1}{s}")
            mine = (q_in[stage - 1, 0] + q_in[stage - 1, 1]) + (q_in[stage - 1, 2] + q_in[stage - 1, 3])
        if axis is None:
            return mine
        slot = q_in.at[stage, at[axis]]
        slot[...] = mine
        for s in (1, 2, 3):
            send(f"q{stage}{s}", slot, slot, device(at, **{axis: s}))

    def products(k, rz):
        col = pl.multiple_of(((z + rz) % 4) * PAIR, 128)
        part = jnp.dot(ct[k * CLS:(k + 1) * CLS, :], f[:, pl.ds(col, PAIR)], preferred_element_type=F32).astype(BF16)
        for px in range(4):
            rx = (px - x + 4) % 4
            for py in range(4):
                ry = (py - y + 4) % 4
                sub = py * 2 + px // 2
                for p in range(3):
                    lane = (px % 2) * ROWS + p * 128
                    piece = part[sub * 64:(sub + 1) * 64, lane:lane + 128]
                    rel = {"x": rx, "y": ry, "z": rz}
                    prod[(p, k) + tuple(rel[a] for a in ORDERS[p])] = piece

    lo, hi = pl.ds(0, 2), pl.ds(2, 2)

    def ring(k, p, m):
        axis = ORDERS[p][0]
        index, part, way = (
            (2, hi, 1), (2, lo, -1), (1, lo, 1), (3, hi, -1), (1, hi, 1), (3, lo, -1))[m]
        send(f"r1{p}{k}{m}", prod.at[p, k, index, part], r1.at[p, k, m], device(at, **{axis: way}))

    def add_ring(k, p):
        for m, index, part in ((0, 1, slice(2, 4)), (1, 3, slice(0, 2))):
            recv(f"r1{p}{k}{m}")
            prod[p, k, index, part] = (
                prod[p, k, index, part].astype(F32) + r1[p, k, m].astype(F32)).astype(BF16)
            ring(k, p, m + 4)

    def end_ring(k, p):
        for m in (2, 3, 4, 5):
            recv(f"r1{p}{k}{m}")
        for part, m, n in ((slice(0, 2), 2, 5), (slice(2, 4), 3, 4)):
            prod[p, k, 0, part] = (
                prod[p, k, 0, part].astype(F32) + r1[p, k, m].astype(F32) + r1[p, k, n].astype(F32)).astype(BF16)
        for s in (2, 1, 3):
            send(f"r2{p}{k}{s}", prod.at[p, k, 0, s], r2.at[p, k, s - 1], device(at, **{ORDERS[p][1]: s}))

    def second(k, p):
        for s in (2, 1, 3):
            recv(f"r2{p}{k}{s}")
        prod[p, k, 0, 0] = (
            prod[p, k, 0, 0].astype(F32) + r2[p, k, 0].astype(F32) + r2[p, k, 1].astype(F32)
            + r2[p, k, 2].astype(F32)).astype(BF16)
        for s in (2, 1, 3):
            send(f"r3{p}{k}{s}", prod.at[p, k, 0, 0, s], r3.at[p, k, s - 1], device(at, **{ORDERS[p][2]: s}))

    mine = y * 2 + xh

    def third(k):
        for p in range(3):
            for s in (2, 1, 3):
                recv(f"r3{p}{k}{s}")
            fin[k, mine, p] = (
                prod[p, k, 0, 0, 0].astype(F32) + r3[p, k, 0].astype(F32) + r3[p, k, 1].astype(F32)
                + r3[p, k, 2].astype(F32)).astype(BF16)
        for dx, dy in ((2, 2), (2, 1), (2, 3), (0, 2), (2, 0), (0, 1), (0, 3)):
            send(f"g{k}{dx}{dy}", fin.at[k, mine], fin.at[k, mine], device(at, x=dx, y=dy))

    def write(k):
        for dx, dy in ((0, 1), (0, 3), (2, 0), (0, 2), (2, 1), (2, 3), (2, 2)):
            recv(f"g{k}{dx}{dy}")
        for p in range(3):
            for j in range(4):
                block = jnp.concatenate([fin[k, 2 * j, p], fin[k, 2 * j + 1, p]], axis=0).astype(F32)
                out[pl.ds(p * 1024 + j * 2 + k, 128, stride=8), :] = block.T

    recv("ct0")
    products(0, 2)
    ring(0, 0, 0)
    ring(0, 0, 1)
    products(0, 3)
    for k, p, m in ((0, 1, 0), (0, 2, 0), (0, 0, 3), (0, 1, 3), (0, 2, 3)):
        ring(k, p, m)
    products(0, 1)
    ring(0, 0, 2)
    products(0, 0)
    for k, p, m in ((0, 1, 1), (0, 2, 1), (0, 1, 2), (0, 2, 2)):
        ring(k, p, m)
    q_stage(1, "z")
    recv("ct1")
    add_ring(0, 0)
    products(1, 2)
    ring(1, 0, 0)
    ring(1, 0, 1)
    add_ring(0, 1)
    add_ring(0, 2)
    products(1, 3)
    for k, p, m in ((1, 1, 0), (1, 2, 0), (1, 0, 3), (1, 1, 3), (1, 2, 3)):
        ring(k, p, m)
    products(1, 1)
    ring(1, 0, 2)
    products(1, 0)
    for k, p, m in ((1, 1, 1), (1, 2, 1), (1, 1, 2), (1, 2, 2)):
        ring(k, p, m)
    q_stage(2, "x")
    for p in range(3):
        end_ring(0, p)
    for p in range(3):
        add_ring(1, p)
    q_stage(3, "y")
    for p in range(3):
        second(0, p)
    for p in range(3):
        end_ring(1, p)
    third(0)
    for p in range(3):
        second(1, p)
    total = q_stage(4, None)
    sums = jnp.sum(total, axis=1, keepdims=True) * inv_count
    quot[...] = jnp.broadcast_to(sums, quot.shape)
    write(0)
    third(1)
    write(1)
    for one in started:
        one.wait_send()


def copies():
    weight = 2 * (1 + 3 + 3)
    chip = 8 + 1 + 1 + 2 + 1
    return weight + chip + 9 + 2 * (3 * (6 + 3 + 3) + 7)


def shards(mesh_size, features, head_weight, probe_seeds):
    all_images = features.shape[0] * mesh_size
    width = features.shape[1]
    loss_scale = 32.0 / math.sqrt(all_images * width)
    vmem = pl.BlockSpec(memory_space=pltpu.VMEM)
    out, quot = pl.pallas_call(
        functools.partial(kernel, loss_scale, 1.0 / (width * CLS)),
        out_shape=(
            jax.ShapeDtypeStruct((ROWS * 8, 128), F32),
            jax.ShapeDtypeStruct((8, 128), F32),
        ),
        in_specs=[pl.BlockSpec(memory_space=pl.ANY), vmem, pl.BlockSpec(memory_space=pltpu.SMEM)],
        out_specs=(vmem, vmem),
        scratch_shapes=[
            pltpu.VMEM((2 * IMG, HALF_D), BF16),
            pltpu.VMEM((2 * CLS, HALF_D), BF16),
            pltpu.VMEM((4, CLS, PAIR), BF16),
            pltpu.VMEM((2, 2 * CLS, IMG), F32),
            pltpu.VMEM((2 * CLS, IMG), F32),
            pltpu.VMEM((2, CLS, IMG), F32),
            pltpu.VMEM((CLS, IMG), F32),
            pltpu.VMEM((2 * CLS, 2 * IMG), BF16),
            pltpu.VMEM((3, 2, 4, 4, 4, 64, 128), BF16),
            pltpu.VMEM((3, 2, 6, 2, 4, 64, 128), BF16),
            pltpu.VMEM((3, 2, 3, 4, 64, 128), BF16),
            pltpu.VMEM((3, 2, 3, 64, 128), BF16),
            pltpu.VMEM((2, 8, 3, 64, 128), BF16),
            pltpu.VMEM((8, 128), F32),
            pltpu.VMEM((4, 4, 8, 128), F32),
            pltpu.SemaphoreType.DMA((8,)),
            pltpu.SemaphoreType.DMA((copies(),)),
            pltpu.SemaphoreType.DMA((copies(),)),
        ],
        compiler_params=pltpu.CompilerParams(
            collective_id=0, has_side_effects=True, vmem_limit_bytes=60 * 1024 * 1024
        ),
        cost_estimate=pl.CostEstimate(flops=16_106_127_360, bytes_accessed=9_000_000, transcendentals=262_144),
    )(features, head_weight, probe_seeds)
    hvp = out.reshape(ROWS, 4, 2, 128).transpose(0, 2, 1, 3).reshape(ROWS, 2, CLS)
    return hvp, quot[:2, 0]


def solution(mesh):
    return jax.shard_map(
        functools.partial(shards, mesh.size),
        mesh=mesh,
        in_specs=(P(("dp", "fsdp"), None), P("fsdp", None), P()),
        out_specs=(P("fsdp", None, None), P()),
        check_vma=False,
    )
```

time: 456 us -> 99.1 us (0.22)
  waiting for transfers between devices: 304 us -> 0 us
  Pallas kernels: 0 us -> 93.9 us
  blocking collectives: 77.4 us -> 0 us
  matrix products: 32 us -> 0 us
  other arithmetic: 17.6 us -> 0 us
  between operations: 15.1 us -> 0.64 us
  local copies, waits for them, and re-layouts: 9.32 us -> 4.39 us
    reduce_scatter x1 -> x0, waiting for transfers between devices: 268 us -> none  [shards(): lax.psum_scatter(lax.dot_general(columns, rounded, (((0,), (0,)), ((), ()...]
    pallas_call x0 -> x1, Pallas kernels: none -> 93.9 us  [shards(): pl.pallas_call(functools.partial(kernel, loss_scale, 1.0 / (width * CLS))...]
    psum x1 -> x0, blocking collectives: 77.4 us -> none  [shards(): quotient = lax.psum(jnp.sum(tangents * curved, axis=(0, 2)), ('dp', 'fsdp'))]
    dot_general x3 -> x0, matrix products: 32 us -> none  [the longest x1 11.8 us: shards(): jnp.dot(features, whole_probes, preferred_element_type=jnp.float32)]
    psum x1 -> x0, waiting for transfers between devices: 18.3 us -> none  [shards(): hvp_rows = lax.psum(group_sum, 'dp')]
    all_gather x1 -> x0, waiting for transfers between devices: 16.9 us -> none  [shards(): lax.all_gather(head_weight, 'fsdp', axis=0, tiled=True)]
    another operation x1 -> x0, other arithmetic: 15.3 us -> none
  transfers between devices with their start and end apart: 3 -> 0, of which waited for: 3 -> 0; matrix products, arithmetic and copies ran while one was open for 6% -> 0% of each run, Pallas kernels for 0% -> 0%
where the time goes in v1:
time: 99.1 us; the launch traced here: 98.9 us
  Pallas kernels  93.9 us (95%)
  local copies, waits for them, and re-layouts  4.39 us (4%)
    pallas_call x1, Pallas kernels, shards(): pl.pallas_call(functools.partial(kernel, loss_scale, 1.0 / (width * CLS))...  93.9 us
    unnamed x1, local copies, waits for them, and re-layouts  3.09 us

profile of v1, /device:TPU:0, one launch (start us, length us, event | category | flops | bytes accessed | tf_op | source)
XLA Modules:
  0.0 98.9 jit_solution(4634840835886004371)
XLA Ops:
  0.6 93.9 %shard_map.50 = (f32[3072,128]{1,0:T(8,128)}, f32[8,128]{1,0:T(8,128)}) custom-call(bf16[512,6144]{1,0:T(8,128)(2,1)} %feat.1, bf16[384,512]{1,0:T(8,128)(2,1)} %head.1, s32[2]{0:T(128)} %seeds.1), custom_call_target="tpu_custom_call" | custom-call | flops 16106127360 | bytes 9000000 | tf_op jit(solution)/shard_map/pallas_call | solution.py:331
  94.5 1.3 %slice_reduce_fusion = f32[2]{0:T(128)} fusion(f32[8,128]{1,0:T(8,128)} %get-tuple-element.5), kind=kLoop, calls=%fused_computation | loop fusion | bytes 16 | tf_op jit(solution)/shard_map/slice | solution.py:365
  95.8 3.1 %copy.8 = f32[384,2,512]{2,1,0:T(2,128)} copy(f32[384,2,512]{2,1,0:T(2,128)} %bitcast.5) | data formatting | bytes 3145728

commit v2 on v1

v2 whole, which is shorter than its diff:
```python
import functools
import math

import jax
import jax.numpy as jnp
from jax import lax
from jax.experimental import pallas as pl
from jax.experimental.pallas import tpu as pltpu
from jax.sharding import PartitionSpec as P

MESH = pl.DeviceIdType.MESH
F32, BF16, I32 = jnp.float32, jnp.bfloat16, jnp.int32
CLS = 512
ROWS = 384
IMG = 512
PAIR = 2 * ROWS
HALF_D = 8 * ROWS
ORDERS = (("z", "x", "y"), ("x", "z", "y"), ("y", "z", "x"))
WRAP_MUL = ((277803737 << 8) + (1 << 31)) % (1 << 32) - (1 << 31)


def place():
    dp, fs = lax.axis_index("dp"), lax.axis_index("fsdp")
    return {"x": (dp & 1) * 2 + ((fs >> 1) & 1), "y": dp >> 1, "z": fs >> 2, "c": fs & 1}


def device(at, **offsets):
    x = (at["x"] + offsets.get("x", 0) + 4) & 3
    y = (at["y"] + offsets.get("y", 0) + 4) & 3
    z = (at["z"] + offsets.get("z", 0) + 4) & 3
    c = (at["c"] + offsets.get("c", 0)) & 1
    return {"dp": y * 2 + (x >> 1), "fsdp": (z * 2 + (x & 1)) * 2 + c}


def contract_last(a, b):
    return lax.dot_general(a, b, (((1,), (1,)), ((), ())), preferred_element_type=F32)


def kernel(
    loss_scale, feat, head, seeds, out, quot,
    f, st, wt, tan, tan_in, log, log_in, ct, prod, r1, r2, r3, fin, q_mine, q_in,
    load_sem, send_sem, recv_sem,
):
    at = place()
    x, y, z, c = at["x"], at["y"], at["z"], at["c"]
    xl, xh = x & 1, x >> 1
    counts = {}
    flying = {}

    def view(part):
        return part[0].at[part[1:]] if isinstance(part, tuple) else part

    def copy(name, src, dst, offsets, q=0, runs=1):
        if name not in counts:
            counts[name] = (sum(n for _, n in counts.values()), runs)
        i = counts[name][0] + q
        return pltpu.make_async_remote_copy(
            src_ref=view(src), dst_ref=view(dst), send_sem=send_sem.at[i], recv_sem=recv_sem.at[i],
            device_id=device(at, **offsets), device_id_type=MESH,
        )

    def send(name, src, dst, **offsets):
        flying[name] = functools.partial(copy, name, src, dst, offsets)
        flying[name]().start()

    def recv(name):
        flying[name]().wait_recv()

    barrier = pltpu.get_barrier_semaphore()
    partners = [{"c": 1}] + [{axis: s} for axis in "xyz" for s in (1, 2, 3)]
    for one in partners:
        pl.semaphore_signal(barrier, inc=1, device_id=device(at, **one), device_id_type=MESH)

    loads = []
    for b in range(8):
        col = pl.multiple_of((2 * b + c) * ROWS, 128)
        one = pltpu.make_async_copy(
            feat.at[:, pl.ds(col, ROWS)], f.at[pl.ds(0, IMG), pl.ds(b * ROWS, ROWS)], load_sem.at[b]
        )
        one.start()
        loads.append(one)

    own_cols = pl.ds(pl.multiple_of(xl * ROWS, 128), ROWS)
    wt[0, :, own_cols] = head[...].T
    log[...] = jnp.zeros_like(log)

    for k in range(2):
        key = seeds[k] * 668265261
        low, high = key & 511, key & ~511
        for b in range(8):
            @pl.loop(0, CLS // 16)
            def _(r):
                d = lax.broadcasted_iota(I32, (16, ROWS), 1) + (2 * b + c) * ROWS
                rows_mixed = ((d * CLS) ^ high) * 747796405 + 289555
                cls = lax.broadcasted_iota(I32, (16, ROWS), 0) + r * 16
                h = rows_mixed + (cls ^ low) * 747796405
                h = (h ^ lax.shift_right_logical(h, 15)) * WRAP_MUL
                h = h ^ (h << 16)
                st[pl.ds(pl.multiple_of(k * CLS + r * 16, 16), 16), b * ROWS:(b + 1) * ROWS] = jnp.where(
                    h < 0, 1.0, -1.0).astype(BF16)

    pl.semaphore_wait(barrier, len(partners))

    def block(rz, q):
        return wt.at[rz, pl.ds(pl.multiple_of(q * 128, 128), 128), own_cols]

    def along_z(s, q):
        return copy(f"wz{s}", block(0, q), block(4 - s, q), {"z": s}, q, 4)

    def across(q, way):
        return copy("wz2", block(2 + way, q), block(2, q), {"z": way}, q, 4)

    def along_x(rz, q):
        return copy("wx", block(rz, q), block(rz, q), {"x": 1 - 2 * (q & 1)}, rz * 4 + q, 16)

    for q in range(4):
        along_z(1, q).start()
        along_z(3, q).start()
        along_x(0, q).start()
    for b in range(8):
        col = pl.multiple_of((2 * b + 1 - c) * ROWS, 128)
        send(f"f{b}", (feat, slice(None), pl.ds(col, ROWS)), (f, pl.ds(IMG, IMG), pl.ds(b * ROWS, ROWS)), c=1)

    for one in loads:
        one.wait()

    @pl.loop(0, 4)
    def _(q):
        @pl.when(q == 2)
        def _():
            for b in range(8):
                recv(f"f{b}")
        rows = pl.ds(pl.multiple_of(q * 256, 256), 256)
        cols = pl.ds(pl.multiple_of((q & 1) * 256, 256), 256)
        tan[q >> 1, :, cols] = contract_last(st[...], f[rows, :])
        along_z(1, q).wait_recv()
        along_z(3, q).wait_recv()
        across(q, 1 - 2 * (q & 1)).start()
        along_x(3, q).start()
        along_x(1, q).start()

    send("tan", (tan, 1), tan_in, c=1)

    @pl.loop(0, 8)
    def _(n):
        j, side = n >> 1, 1 - (n & 1)
        rz = j ^ (j >> 1)

        @pl.when(n == 2)
        def _():
            @pl.loop(0, 4)
            def _(q):
                across(q, 1).wait_recv()
                along_x(2, q).start()

        @pl.when((n & 1) == 0)
        def _():
            for q in range(4):
                along_x(rz, q).wait_recv()

        col = pl.multiple_of(((z + rz) & 3) * PAIR, 128)
        rows = pl.ds(pl.multiple_of(side * IMG, IMG), IMG)
        log[side] += contract_last(wt[rz], f[rows, pl.ds(col, PAIR)])

        @pl.when(n == 6)
        def _():
            send("log", (log, 1), log_in, c=1)

    recv("tan")
    recv("log")

    @pl.loop(0, 4)
    def _(t):
        cols = pl.ds(pl.multiple_of(t * 128, 128), 128)
        total = log[0, :, cols] + log_in[:, cols]
        e = jnp.exp(total - jnp.max(total, axis=0, keepdims=True))
        log[0, :, cols] = e * (1.0 / jnp.sum(e, axis=0, keepdims=True))

    q_mine[...] = jnp.zeros_like(q_mine)

    @pl.loop(0, 8)
    def _(n):
        k, t = n >> 2, n & 3
        cols = pl.ds(pl.multiple_of(t * 128, 128), 128)
        rows = pl.ds(pl.multiple_of(k * CLS, CLS), CLS)
        chances = log[0, :, cols]
        tangent = tan[0, rows, cols] + tan_in[rows, cols]
        centre = jnp.sum(chances * tangent, axis=0, keepdims=True)
        curved = loss_scale * chances * (tangent - centre)
        q_mine[pl.ds(k, 1), :] += jnp.sum(tangent * curved, axis=0, keepdims=True)
        ct[rows, cols] = curved.astype(BF16)

        for kk in range(2):
            @pl.when(n == kk * 4 + 3)
            def _():
                rows = pl.ds(kk * CLS, CLS)
                send(f"ct{kk}", (ct, rows, pl.ds(0, IMG)), (ct, rows, pl.ds(IMG, IMG)), c=1)

    send("qc", q_mine, (q_in, 0, 0), c=1)

    def q_stage(stage, axis):
        if stage == 1:
            recv("qc")
            mine = q_mine[...] + q_in[0, 0]
        else:
            for s in (1, 2, 3):
                recv(f"q{stage - 1}{s}")
            mine = (q_in[stage - 1, 0] + q_in[stage - 1, 1]) + (q_in[stage - 1, 2] + q_in[stage - 1, 3])
        if axis is None:
            return mine
        q_in[stage, at[axis]] = mine
        slot = (q_in, stage, at[axis])
        for s in (1, 2, 3):
            send(f"q{stage}{s}", slot, slot, **{axis: s})

    def products(k, rz):
        col = pl.multiple_of(((z + rz) & 3) * PAIR, 128)
        rows = pl.ds(pl.multiple_of(k * CLS, CLS), CLS)
        part = jnp.dot(ct[rows, :], f[:, pl.ds(col, PAIR)], preferred_element_type=F32).astype(BF16)
        for px in range(4):
            rx = (px - x + 4) & 3
            for py in range(4):
                ry = (py - y + 4) & 3
                sub = py * 2 + px // 2
                for p in range(3):
                    lane = (px % 2) * ROWS + p * 128
                    piece = part[sub * 64:(sub + 1) * 64, lane:lane + 128]
                    rel = {"x": rx, "y": ry, "z": rz}
                    prod[(p, k) + tuple(rel[a] for a in ORDERS[p])] = piece

    lo, hi = pl.ds(0, 2), pl.ds(2, 2)

    def ring(k, p, m):
        index, part, way = (
            (2, hi, 1), (2, lo, -1), (1, lo, 1), (3, hi, -1), (1, hi, 1), (3, lo, -1))[m]
        send(f"r1{p}{k}{m}", (prod, p, k, index, part), (r1, p, k, m), **{ORDERS[p][0]: way})

    def add_ring(k, p):
        for m, index, part in ((0, 1, slice(2, 4)), (1, 3, slice(0, 2))):
            recv(f"r1{p}{k}{m}")
            prod[p, k, index, part] = (
                prod[p, k, index, part].astype(F32) + r1[p, k, m].astype(F32)).astype(BF16)
            ring(k, p, m + 4)

    def end_ring(k, p):
        for m in (2, 3, 4, 5):
            recv(f"r1{p}{k}{m}")
        for part, m, n in ((slice(0, 2), 2, 5), (slice(2, 4), 3, 4)):
            prod[p, k, 0, part] = (
                prod[p, k, 0, part].astype(F32) + r1[p, k, m].astype(F32) + r1[p, k, n].astype(F32)).astype(BF16)
        for s in (2, 1, 3):
            send(f"r2{p}{k}{s}", (prod, p, k, 0, s), (r2, p, k, s - 1), **{ORDERS[p][1]: s})

    def second(k, p):
        for s in (2, 1, 3):
            recv(f"r2{p}{k}{s}")
        prod[p, k, 0, 0] = (
            prod[p, k, 0, 0].astype(F32) + r2[p, k, 0].astype(F32) + r2[p, k, 1].astype(F32)
            + r2[p, k, 2].astype(F32)).astype(BF16)
        for s in (2, 1, 3):
            send(f"r3{p}{k}{s}", (prod, p, k, 0, 0, s), (r3, p, k, s - 1), **{ORDERS[p][2]: s})

    mine = y * 2 + xh
    twin = y * 2 + 1 - xh

    def third(k):
        for p in range(3):
            for s in (2, 1, 3):
                recv(f"r3{p}{k}{s}")
            fin[k, mine, p] = (
                prod[p, k, 0, 0, 0].astype(F32) + r3[p, k, 0].astype(F32) + r3[p, k, 1].astype(F32)
                + r3[p, k, 2].astype(F32)).astype(BF16)
        slot = (fin, k, mine)
        send(f"gx{k}", slot, slot, x=2)
        for s in (2, 1, 3):
            send(f"ga{k}{s}", slot, slot, y=s)

    def relay(k):
        recv(f"gx{k}")
        slot = (fin, k, twin)
        for s in (2, 1, 3):
            send(f"gb{k}{s}", slot, slot, y=s)

    def write(k):
        for s in (1, 3, 2):
            recv(f"ga{k}{s}")
        for s in (1, 3, 2):
            recv(f"gb{k}{s}")
        out[k] = fin[k]

    @pl.loop(0, 8)
    def _(n):
        for k in range(2):
            @pl.when(n == k * 4)
            def _():
                recv(f"ct{k}")

        products(n >> 2, (n + 2) & 3)
        for k in range(2):
            @pl.when(n == k * 4)
            def _():
                ring(k, 0, 0)
                ring(k, 0, 1)

            @pl.when(n == k * 4 + 1)
            def _():
                for p, m in ((1, 0), (2, 0), (0, 3), (1, 3), (2, 3)):
                    ring(k, p, m)

            @pl.when(n == k * 4 + 3)
            def _():
                for p, m in ((1, 1), (2, 1), (0, 2), (1, 2), (2, 2)):
                    ring(k, p, m)

        @pl.when(n == 4)
        def _():
            q_stage(1, "z")
            add_ring(0, 0)

        @pl.when(n == 5)
        def _():
            add_ring(0, 1)
            add_ring(0, 2)

    q_stage(2, "x")
    for p in range(3):
        end_ring(0, p)
    for p in range(3):
        add_ring(1, p)
    q_stage(3, "y")
    for p in range(3):
        second(0, p)
    for p in range(3):
        end_ring(1, p)
    third(0)
    for p in range(3):
        second(1, p)
    relay(0)
    quot[...] = q_stage(4, None)
    third(1)
    write(0)
    relay(1)
    write(1)

    @pl.loop(0, 4)
    def _(q):
        along_z(1, q).wait_send()
        along_z(3, q).wait_send()
        across(q, 1 - 2 * (q & 1)).wait_send()
        for rz in range(4):
            along_x(rz, q).wait_send()

    for one in flying.values():
        one().wait_send()


def unpack(inv_count, sums, quot_in, out, quot):
    for k in range(2):
        quot[k] = jnp.sum(quot_in[k:k + 1, :]) * inv_count
        for p in range(3):
            for j in range(4):
                block = sums[k, 2 * j:2 * j + 2, p].reshape(128, 128).astype(F32)
                out[pl.ds(p * 1024 + j * 2 + k, 128, stride=8), :] = block.T


def copies():
    weight = 4 * (1 + 3 + 3)
    chip = 8 + 1 + 1 + 2 + 1
    return weight + chip + 9 + 2 * (3 * (6 + 3 + 3) + 7)


def shards(mesh_size, features, head_weight, probe_seeds):
    all_images = features.shape[0] * mesh_size
    width = features.shape[1]
    loss_scale = 32.0 / math.sqrt(all_images * width)
    vmem = pl.BlockSpec(memory_space=pltpu.VMEM)
    sums, total = pl.pallas_call(
        functools.partial(kernel, loss_scale),
        out_shape=(
            jax.ShapeDtypeStruct((2, 8, 3, 64, 128), BF16),
            jax.ShapeDtypeStruct((8, 128), F32),
        ),
        in_specs=[pl.BlockSpec(memory_space=pl.ANY), vmem, pl.BlockSpec(memory_space=pltpu.SMEM)],
        out_specs=(vmem, vmem),
        scratch_shapes=[
            pltpu.VMEM((2 * IMG, HALF_D), BF16),
            pltpu.VMEM((2 * CLS, HALF_D), BF16),
            pltpu.VMEM((4, CLS, PAIR), BF16),
            pltpu.VMEM((2, 2 * CLS, IMG), F32),
            pltpu.VMEM((2 * CLS, IMG), F32),
            pltpu.VMEM((2, CLS, IMG), F32),
            pltpu.VMEM((CLS, IMG), F32),
            pltpu.VMEM((2 * CLS, 2 * IMG), BF16),
            pltpu.VMEM((3, 2, 4, 4, 4, 64, 128), BF16),
            pltpu.VMEM((3, 2, 6, 2, 4, 64, 128), BF16),
            pltpu.VMEM((3, 2, 3, 4, 64, 128), BF16),
            pltpu.VMEM((3, 2, 3, 64, 128), BF16),
            pltpu.VMEM((2, 8, 3, 64, 128), BF16),
            pltpu.VMEM((8, 128), F32),
            pltpu.VMEM((4, 4, 8, 128), F32),
            pltpu.SemaphoreType.DMA((8,)),
            pltpu.SemaphoreType.DMA((copies(),)),
            pltpu.SemaphoreType.DMA((copies(),)),
        ],
        compiler_params=pltpu.CompilerParams(
            collective_id=0, has_side_effects=True, vmem_limit_bytes=60 * 1024 * 1024
        ),
        cost_estimate=pl.CostEstimate(flops=16_106_127_360, bytes_accessed=9_000_000, transcendentals=262_144),
    )(features, head_weight, probe_seeds)
    out, quot = pl.pallas_call(
        functools.partial(unpack, 1.0 / (width * CLS)),
        out_shape=(jax.ShapeDtypeStruct((ROWS * 8, 128), F32), jax.ShapeDtypeStruct((2,), F32)),
        in_specs=[vmem, vmem],
        out_specs=(vmem, pl.BlockSpec(memory_space=pltpu.SMEM)),
    )(sums, total)
    hvp = out.reshape(ROWS, 4, 2, 128).transpose(0, 2, 1, 3).reshape(ROWS, 2, CLS)
    return hvp, quot


def solution(mesh):
    return jax.shard_map(
        functools.partial(shards, mesh.size),
        mesh=mesh,
        in_specs=(P(("dp", "fsdp"), None), P("fsdp", None), P()),
        out_specs=(P("fsdp", None, None), P()),
        check_vma=False,
    )
```

time: 99.1 us -> 93 us (0.938)
  local copies, waits for them, and re-layouts: 4.39 us -> 0 us
  Pallas kernels: 93.9 us -> 92.2 us
    unnamed x1 -> x0, local copies, waits for them, and re-layouts: 3.09 us -> none
    pallas_call x1 -> x2, Pallas kernels: 93.9 us -> 92.2 us  [the longest x1 89.6 us: shards(): pl.pallas_call(functools.partial(kernel, loss_scale), out_shape=(jax.Shap...]
    slice x1 -> x0, local copies, waits for them, and re-layouts: 1.3 us -> none  [shards(): return (hvp, quot[:2, 0])]
where the time goes in v2:
time: 93 us; the launch traced here: 92.9 us
  Pallas kernels  92.2 us (99%)
    pallas_call x1, Pallas kernels, shards(): pl.pallas_call(functools.partial(kernel, loss_scale), out_shape=(jax.Shap...  89.6 us
    pallas_call x1, Pallas kernels, shards(): pl.pallas_call(functools.partial(unpack, 1.0 / (width * CLS)), out_shape=...  2.6 us

profile of v2, /device:TPU:0, one launch (start us, length us, event | category | flops | bytes accessed | tf_op | source)
XLA Modules:
  0.0 92.9 jit_solution(9313676462308085851)
XLA Ops:
  0.6 89.6 %shard_map.50 = (bf16[2,8,3,64,128]{4,3,2,1,0:T(8,128)(2,1)}, f32[8,128]{1,0:T(8,128)}) custom-call(bf16[512,6144]{1,0:T(8,128)(2,1)} %feat.1, bf16[384,512]{1,0:T(8,128)(2,1)} %head.1, s32[2]{0:T(128)} %seeds.1), custom_call_target="tpu_custom_call" | custom-call | flops 16106127360 | bytes 9000000 | tf_op jit(solution)/shard_map/pallas_call | solution.py:377
  90.3 2.6 %shard_map.51 = (f32[3072,128]{1,0:T(8,128)}, f32[2]{0:T(128)}) custom-call(bf16[2,8,3,64,128]{4,3,2,1,0:T(8,128)(2,1)} %get-tuple-element.6.sums, f32[8,128]{1,0:T(8,128)} %get-tuple-element.7.quot_in), custom_call_target="tpu_custom_call" | custom-call | tf_op jit(solution)/shard_map/pallas_call | solution.py:410

commit v3 on v2

--- a/solution.py
+++ b/solution.py
@@ -15,7 +15,7 @@
 IMG = 512
 PAIR = 2 * ROWS
 HALF_D = 8 * ROWS
-ORDERS = (("z", "x", "y"), ("x", "z", "y"), ("y", "z", "x"))
+ORDERS = (("z", "x", "y"), ("x", "y", "z"), ("y", "z", "x"))
 WRAP_MUL = ((277803737 << 8) + (1 << 31)) % (1 << 32) - (1 << 31)
 
 
@@ -38,33 +38,37 @@
 
 def kernel(
     loss_scale, feat, head, seeds, out, quot,
-    f, st, wt, tan, tan_in, log, log_in, ct, prod, r1, r2, r3, fin, q_mine, q_in,
+    f, st, wt, tan, tan_in, log, log_in, ct, prod, r1, r1b, r2, r3, fin, q_mine, q_in,
     load_sem, send_sem, recv_sem,
 ):
     at = place()
     x, y, z, c = at["x"], at["y"], at["z"], at["c"]
     xl, xh = x & 1, x >> 1
-    counts = {}
-    flying = {}
+    waits = {}
 
     def view(part):
         return part[0].at[part[1:]] if isinstance(part, tuple) else part
 
-    def copy(name, src, dst, offsets, q=0, runs=1):
-        if name not in counts:
-            counts[name] = (sum(n for _, n in counts.values()), runs)
-        i = counts[name][0] + q
+    def sem_of(kind, name):
+        names = waits.setdefault(kind, [])
+        if name not in names:
+            names.append(name)
+        return names.index(name)
+
+    def copy(got, gone, src, dst, offsets):
         return pltpu.make_async_remote_copy(
-            src_ref=view(src), dst_ref=view(dst), send_sem=send_sem.at[i], recv_sem=recv_sem.at[i],
-            device_id=device(at, **offsets), device_id_type=MESH,
+            src_ref=view(src), dst_ref=view(dst), send_sem=send_sem.at[sem_of("gone", gone)],
+            recv_sem=recv_sem.at[sem_of("got", got)], device_id=device(at, **offsets), device_id_type=MESH,
         )
 
-    def send(name, src, dst, **offsets):
-        flying[name] = functools.partial(copy, name, src, dst, offsets)
-        flying[name]().start()
-
-    def recv(name):
-        flying[name]().wait_recv()
+    def send(got, gone, src, dst, **offsets):
+        copy(got, gone, src, dst, offsets).start()
+
+    def recv(got, whole):
+        copy(got, waits["gone"][0], whole, whole, {"c": 1}).wait_recv()
+
+    def drain(gone, whole):
+        copy(waits["got"][0], gone, whole, whole, {"c": 1}).wait_send()
 
     barrier = pltpu.get_barrier_semaphore()
     partners = [{"c": 1}] + [{axis: s} for axis in "xyz" for s in (1, 2, 3)]
@@ -81,10 +85,11 @@
         loads.append(one)
 
     own_cols = pl.ds(pl.multiple_of(xl * ROWS, 128), ROWS)
+    other_cols = pl.ds(pl.multiple_of((1 - xl) * ROWS, 128), ROWS)
     wt[0, :, own_cols] = head[...].T
     log[...] = jnp.zeros_like(log)
 
-    for k in range(2):
+    def signs(k):
         key = seeds[k] * 668265261
         low, high = key & 511, key & ~511
         for b in range(8):
@@ -99,47 +104,55 @@
                 st[pl.ds(pl.multiple_of(k * CLS + r * 16, 16), 16), b * ROWS:(b + 1) * ROWS] = jnp.where(
                     h < 0, 1.0, -1.0).astype(BF16)
 
+    signs(0)
+    signs(1)
     pl.semaphore_wait(barrier, len(partners))
 
     def block(rz, q):
-        return wt.at[rz, pl.ds(pl.multiple_of(q * 128, 128), 128), own_cols]
+        return wt, rz, pl.ds(pl.multiple_of(q * 128, 128), 128), own_cols
 
     def along_z(s, q):
-        return copy(f"wz{s}", block(0, q), block(4 - s, q), {"z": s}, q, 4)
-
-    def across(q, way):
-        return copy("wz2", block(2 + way, q), block(2, q), {"z": way}, q, 4)
+        send(f"wz{s}{q}", "wz", block(0, q), block(4 - s, q), z=s)
 
     def along_x(rz, q):
-        return copy("wx", block(rz, q), block(rz, q), {"x": 1 - 2 * (q & 1)}, rz * 4 + q, 16)
-
-    for q in range(4):
-        along_z(1, q).start()
-        along_z(3, q).start()
-        along_x(0, q).start()
+        send(f"wx{rz}", "wx", block(rz, q), block(rz, q), x=1 - 2 * (q % 2))
+
+    def own_block(q):
+        along_z(1, q)
+        along_z(3, q)
+        along_x(0, q)
+
+    own_block(0)
     for b in range(8):
         col = pl.multiple_of((2 * b + 1 - c) * ROWS, 128)
-        send(f"f{b}", (feat, slice(None), pl.ds(col, ROWS)), (f, pl.ds(IMG, IMG), pl.ds(b * ROWS, ROWS)), c=1)
-
+        send("f", "f", (feat, slice(None), pl.ds(col, ROWS)), (f, pl.ds(IMG, IMG), pl.ds(b * ROWS, ROWS)), c=1)
+
+    own_block(1)
     for one in loads:
         one.wait()
 
     @pl.loop(0, 4)
-    def _(q):
-        @pl.when(q == 2)
+    def _(n):
+        @pl.when(n == 2)
         def _():
-            for b in range(8):
-                recv(f"f{b}")
-        rows = pl.ds(pl.multiple_of(q * 256, 256), 256)
-        cols = pl.ds(pl.multiple_of((q & 1) * 256, 256), 256)
-        tan[q >> 1, :, cols] = contract_last(st[...], f[rows, :])
-        along_z(1, q).wait_recv()
-        along_z(3, q).wait_recv()
-        across(q, 1 - 2 * (q & 1)).start()
-        along_x(3, q).start()
-        along_x(1, q).start()
-
-    send("tan", (tan, 1), tan_in, c=1)
+            recv("f", (f, pl.ds(IMG, IMG)))
+        rows = pl.ds(pl.multiple_of(n * 256, 256), 256)
+        cols = pl.ds(pl.multiple_of((n & 1) * 256, 256), 256)
+        tan[n >> 1, :, cols] = contract_last(st[...], f[rows, :])
+
+        for q in range(4):
+            @pl.when(n == q)
+            def _():
+                if q < 2:
+                    own_block(q + 2)
+                for s in (1, 3):
+                    recv(f"wz{s}{q}", block(4 - s, q))
+                way = 1 - 2 * (q % 2)
+                send(f"wzz{q}", "wzz", block(2 + way, q), block(2, q), z=way)
+                along_x(3, q)
+                along_x(1, q)
+
+    send("tan", "tan", (tan, 1), tan_in, c=1)
 
     @pl.loop(0, 8)
     def _(n):
@@ -148,15 +161,14 @@
 
         @pl.when(n == 2)
         def _():
-            @pl.loop(0, 4)
-            def _(q):
-                across(q, 1).wait_recv()
-                along_x(2, q).start()
-
-        @pl.when((n & 1) == 0)
-        def _():
             for q in range(4):
-                along_x(rz, q).wait_recv()
+                recv(f"wzz{q}", block(2, q))
+                along_x(2, q)
+
+        for jj, block_of in enumerate((0, 1, 3, 2)):
+            @pl.when(n == 2 * jj)
+            def _():
+                recv(f"wx{block_of}", (wt, block_of, slice(None), other_cols))
 
         col = pl.multiple_of(((z + rz) & 3) * PAIR, 128)
         rows = pl.ds(pl.multiple_of(side * IMG, IMG), IMG)
@@ -164,10 +176,10 @@
 
         @pl.when(n == 6)
         def _():
-            send("log", (log, 1), log_in, c=1)
-
-    recv("tan")
-    recv("log")
+            send("log", "log", (log, 1), log_in, c=1)
+
+    recv("tan", tan_in)
+    recv("log", log_in)
 
     @pl.loop(0, 4)
     def _(t):
@@ -194,24 +206,23 @@
             @pl.when(n == kk * 4 + 3)
             def _():
                 rows = pl.ds(kk * CLS, CLS)
-                send(f"ct{kk}", (ct, rows, pl.ds(0, IMG)), (ct, rows, pl.ds(IMG, IMG)), c=1)
-
-    send("qc", q_mine, (q_in, 0, 0), c=1)
+                send(f"ct{kk}", f"ct{kk}", (ct, rows, pl.ds(0, IMG)), (ct, rows, pl.ds(IMG, IMG)), c=1)
+
+    send("qc", "qc", q_mine, (q_in, 0, 0), c=1)
 
     def q_stage(stage, axis):
         if stage == 1:
-            recv("qc")
+            recv("qc", (q_in, 0, 0))
             mine = q_mine[...] + q_in[0, 0]
         else:
-            for s in (1, 2, 3):
-                recv(f"q{stage - 1}{s}")
+            recv(f"q{stage - 1}", (q_in, stage - 1, pl.ds(0, 3)))
             mine = (q_in[stage - 1, 0] + q_in[stage - 1, 1]) + (q_in[stage - 1, 2] + q_in[stage - 1, 3])
         if axis is None:
             return mine
         q_in[stage, at[axis]] = mine
         slot = (q_in, stage, at[axis])
         for s in (1, 2, 3):
-            send(f"q{stage}{s}", slot, slot, **{axis: s})
+            send(f"q{stage}", f"q{stage}", slot, slot, **{axis: s})
 
     def products(k, rz):
         col = pl.multiple_of(((z + rz) & 3) * PAIR, 128)
@@ -228,64 +239,77 @@
                     rel = {"x": rx, "y": ry, "z": rz}
                     prod[(p, k) + tuple(rel[a] for a in ORDERS[p])] = piece
 
-    lo, hi = pl.ds(0, 2), pl.ds(2, 2)
+    def half(k, p, index, upper):
+        cut = pl.ds(2, 2) if upper else pl.ds(0, 2)
+        return (prod, p, k, index, slice(None), cut) if p == 1 else (prod, p, k, index, cut)
+
+    def arrived(k, p, m):
+        return (r1b, k, m) if p == 1 else (r1, p // 2, k, m)
 
     def ring(k, p, m):
-        index, part, way = (
-            (2, hi, 1), (2, lo, -1), (1, lo, 1), (3, hi, -1), (1, hi, 1), (3, lo, -1))[m]
-        send(f"r1{p}{k}{m}", (prod, p, k, index, part), (r1, p, k, m), **{ORDERS[p][0]: way})
+        index, upper, way = (
+            (2, True, 1), (2, False, -1), (1, False, 1), (3, True, -1), (1, True, 1), (3, False, -1))[m]
+        send(f"r1{p}{k}{min(m, 2)}", f"r1{p}{k}", half(k, p, index, upper), arrived(k, p, m), **{ORDERS[p][0]: way})
+
+    def add(target, *parts):
+        total = view(target)[...].astype(F32)
+        for part in parts:
+            total += view(part)[...].astype(F32)
+        view(target)[...] = total.astype(BF16)
 
     def add_ring(k, p):
-        for m, index, part in ((0, 1, slice(2, 4)), (1, 3, slice(0, 2))):
-            recv(f"r1{p}{k}{m}")
-            prod[p, k, index, part] = (
-                prod[p, k, index, part].astype(F32) + r1[p, k, m].astype(F32)).astype(BF16)
+        for m, index, upper in ((0, 1, True), (1, 3, False)):
+            recv(f"r1{p}{k}{m}", arrived(k, p, m))
+            add(half(k, p, index, upper), arrived(k, p, m))
             ring(k, p, m + 4)
 
     def end_ring(k, p):
-        for m in (2, 3, 4, 5):
-            recv(f"r1{p}{k}{m}")
-        for part, m, n in ((slice(0, 2), 2, 5), (slice(2, 4), 3, 4)):
-            prod[p, k, 0, part] = (
-                prod[p, k, 0, part].astype(F32) + r1[p, k, m].astype(F32) + r1[p, k, n].astype(F32)).astype(BF16)
+        recv(f"r1{p}{k}2", arrived(k, p, pl.ds(2, 4)))
+        for upper, m, n in ((False, 2, 5), (True, 3, 4)):
+            add(half(k, p, 0, upper), arrived(k, p, m), arrived(k, p, n))
         for s in (2, 1, 3):
-            send(f"r2{p}{k}{s}", (prod, p, k, 0, s), (r2, p, k, s - 1), **{ORDERS[p][1]: s})
+            send(f"r2{p}{k}", f"r2{p}{k}", (prod, p, k, 0, s), (r2, p, k, s - 1), **{ORDERS[p][1]: s})
 
     def second(k, p):
-        for s in (2, 1, 3):
-            recv(f"r2{p}{k}{s}")
+        recv(f"r2{p}{k}", (r2, p, k))
         prod[p, k, 0, 0] = (
             prod[p, k, 0, 0].astype(F32) + r2[p, k, 0].astype(F32) + r2[p, k, 1].astype(F32)
             + r2[p, k, 2].astype(F32)).astype(BF16)
         for s in (2, 1, 3):
-            send(f"r3{p}{k}{s}", (prod, p, k, 0, 0, s), (r3, p, k, s - 1), **{ORDERS[p][2]: s})
+            send(f"r3{k}", f"r3{k}", (prod, p, k, 0, 0, s), (r3, p, k, s - 1), **{ORDERS[p][2]: s})
 
     mine = y * 2 + xh
-    twin = y * 2 + 1 - xh
+
+    def spot(k, dx, dy):
+        return fin, k, ((y + dy) & 3) * 2 + ((xh + dx) & 1)
 
     def third(k):
+        recv(f"r3{k}", (r3, slice(None), k))
         for p in range(3):
-            for s in (2, 1, 3):
-                recv(f"r3{p}{k}{s}")
             fin[k, mine, p] = (
                 prod[p, k, 0, 0, 0].astype(F32) + r3[p, k, 0].astype(F32) + r3[p, k, 1].astype(F32)
                 + r3[p, k, 2].astype(F32)).astype(BF16)
-        slot = (fin, k, mine)
-        send(f"gx{k}", slot, slot, x=2)
+        slot = spot(k, 0, 0)
+        send(f"gx{k}", f"g{k}", slot, slot, x=2)
         for s in (2, 1, 3):
-            send(f"ga{k}{s}", slot, slot, y=s)
+            send(f"gy{k}", f"g{k}", slot, slot, y=s)
 
     def relay(k):
-        recv(f"gx{k}")
-        slot = (fin, k, twin)
-        for s in (2, 1, 3):
-            send(f"gb{k}{s}", slot, slot, y=s)
+        if k == 0:
+            recv("gy0", (fin, k, pl.ds(0, 3)))
+            for s in (1, 3, 2):
+                send("gz0", "g0", spot(k, 0, s), spot(k, 0, s), x=2)
+        else:
+            recv("gx1", spot(k, 1, 0))
+            for s in (2, 1, 3):
+                send("gz1", "g1", spot(k, 1, 0), spot(k, 1, 0), y=s)
 
     def write(k):
-        for s in (1, 3, 2):
-            recv(f"ga{k}{s}")
-        for s in (1, 3, 2):
-            recv(f"gb{k}{s}")
+        if k == 0:
+            recv("gx0", spot(k, 1, 0))
+        else:
+            recv("gy1", (fin, k, pl.ds(0, 3)))
+        recv(f"gz{k}", (fin, k, pl.ds(0, 3)))
         out[k] = fin[k]
 
     @pl.loop(0, 8)
@@ -293,7 +317,7 @@
         for k in range(2):
             @pl.when(n == k * 4)
             def _():
-                recv(f"ct{k}")
+                recv(f"ct{k}", (ct, pl.ds(k * CLS, CLS), pl.ds(IMG, IMG)))
 
         products(n >> 2, (n + 2) & 3)
         for k in range(2):
@@ -342,16 +366,22 @@
     relay(1)
     write(1)
 
-    @pl.loop(0, 4)
-    def _(q):
-        along_z(1, q).wait_send()
-        along_z(3, q).wait_send()
-        across(q, 1 - 2 * (q & 1)).wait_send()
-        for rz in range(4):
-            along_x(rz, q).wait_send()
-
-    for one in flying.values():
-        one().wait_send()
+    drain("wz", (wt, pl.ds(0, 2), slice(None), own_cols))
+    drain("wzz", (wt, 0, slice(None), own_cols))
+    drain("wx", (wt, slice(None), slice(None), own_cols))
+    drain("f", (f, pl.ds(IMG, IMG)))
+    drain("tan", tan_in)
+    drain("log", log_in)
+    drain("qc", q_mine)
+    for stage in (1, 2, 3):
+        drain(f"q{stage}", (q_in, stage, pl.ds(0, 3)))
+    for k in range(2):
+        drain(f"ct{k}", (ct, pl.ds(k * CLS, CLS), pl.ds(0, IMG)))
+        for p in range(3):
+            drain(f"r1{p}{k}", (prod, p, k, pl.ds(0, 3)))
+            drain(f"r2{p}{k}", (r2, p, k))
+        drain(f"r3{k}", (r3, slice(None), k))
+        drain(f"g{k}", (fin, k, pl.ds(0, 7)))
 
 
 def unpack(inv_count, sums, quot_in, out, quot):
@@ -361,12 +391,6 @@
             for j in range(4):
                 block = sums[k, 2 * j:2 * j + 2, p].reshape(128, 128).astype(F32)
                 out[pl.ds(p * 1024 + j * 2 + k, 128, stride=8), :] = block.T
-
-
-def copies():
-    weight = 4 * (1 + 3 + 3)
-    chip = 8 + 1 + 1 + 2 + 1
-    return weight + chip + 9 + 2 * (3 * (6 + 3 + 3) + 7)
 
 
 def shards(mesh_size, features, head_weight, probe_seeds):
@@ -392,15 +416,16 @@
             pltpu.VMEM((CLS, IMG), F32),
             pltpu.VMEM((2 * CLS, 2 * IMG), BF16),
             pltpu.VMEM((3, 2, 4, 4, 4, 64, 128), BF16),
-            pltpu.VMEM((3, 2, 6, 2, 4, 64, 128), BF16),
+            pltpu.VMEM((2, 2, 6, 2, 4, 64, 128), BF16),
+            pltpu.VMEM((2, 6, 4, 2, 64, 128), BF16),
             pltpu.VMEM((3, 2, 3, 4, 64, 128), BF16),
             pltpu.VMEM((3, 2, 3, 64, 128), BF16),
             pltpu.VMEM((2, 8, 3, 64, 128), BF16),
             pltpu.VMEM((8, 128), F32),
             pltpu.VMEM((4, 4, 8, 128), F32),
             pltpu.SemaphoreType.DMA((8,)),
-            pltpu.SemaphoreType.DMA((copies(),)),
-            pltpu.SemaphoreType.DMA((copies(),)),
+            pltpu.SemaphoreType.DMA((28,)),
+            pltpu.SemaphoreType.DMA((57,)),
         ],
         compiler_params=pltpu.CompilerParams(
             collective_id=0, has_side_effects=True, vmem_limit_bytes=60 * 1024 * 1024

time: 93 us -> 91 us (0.978)
  Pallas kernels: 92.2 us -> 90.1 us
    pallas_call x1, Pallas kernels: 89.6 us -> 87.5 us  [shards(): pl.pallas_call(functools.partial(kernel, loss_scale), out_shape=(jax.Shap...]
where the time goes in v3:
time: 91 us; the launch traced here: 90.8 us
  Pallas kernels  90.1 us (99%)
    pallas_call x1, Pallas kernels, shards(): pl.pallas_call(functools.partial(kernel, loss_scale), out_shape=(jax.Shap...  87.5 us
    pallas_call x1, Pallas kernels, shards(): pl.pallas_call(functools.partial(unpack, 1.0 / (width * CLS)), out_shape=...  2.6 us

profile of v3, /device:TPU:0, one launch (start us, length us, event | category | flops | bytes accessed | tf_op | source)
XLA Modules:
  0.0 90.8 jit_solution(18180959067780753520)
XLA Ops:
  0.6 87.5 %shard_map.50 = (bf16[2,8,3,64,128]{4,3,2,1,0:T(8,128)(2,1)}, f32[8,128]{1,0:T(8,128)}) custom-call(bf16[512,6144]{1,0:T(8,128)(2,1)} %feat.1, bf16[384,512]{1,0:T(8,128)(2,1)} %head.1, s32[2]{0:T(128)} %seeds.1), custom_call_target="tpu_custom_call" | custom-call | flops 16106127360 | bytes 9000000 | tf_op jit(solution)/shard_map/pallas_call | solution.py:401
  88.2 2.6 %shard_map.51 = (f32[3072,128]{1,0:T(8,128)}, f32[2]{0:T(128)}) custom-call(bf16[2,8,3,64,128]{4,3,2,1,0:T(8,128)(2,1)} %get-tuple-element.6.sums, f32[8,128]{1,0:T(8,128)} %get-tuple-element.7.quot_in), custom_call_target="tpu_custom_call" | custom-call | tf_op jit(solution)/shard_map/pallas_call | solution.py:435

commit v4 on v3

--- a/solution.py
+++ b/solution.py
@@ -348,9 +348,8 @@
 
     q_stage(2, "x")
     for p in range(3):
+        add_ring(1, p)
         end_ring(0, p)
-    for p in range(3):
-        add_ring(1, p)
     q_stage(3, "y")
     for p in range(3):
         second(0, p)

time: 91 us -> 93.2 us (1.024)
  Pallas kernels: 90.1 us -> 91.6 us
    pallas_call x1, Pallas kernels: 87.5 us -> 89 us  [shards(): pl.pallas_call(functools.partial(kernel, loss_scale), out_shape=(jax.Shap...]
where the time goes in v4:
time: 93.2 us; the launch traced here: 92.2 us
  Pallas kernels  91.6 us (98%)
    pallas_call x1, Pallas kernels, shards(): pl.pallas_call(functools.partial(kernel, loss_scale), out_shape=(jax.Shap...  89 us
    pallas_call x1, Pallas kernels, shards(): pl.pallas_call(functools.partial(unpack, 1.0 / (width * CLS)), out_shape=...  2.6 us

profile of v4, /device:TPU:0, one launch (start us, length us, event | category | flops | bytes accessed | tf_op | source)
XLA Modules:
  0.0 92.2 jit_solution(16244658132842068506)
XLA Ops:
  0.6 89.0 %shard_map.50 = (bf16[2,8,3,64,128]{4,3,2,1,0:T(8,128)(2,1)}, f32[8,128]{1,0:T(8,128)}) custom-call(bf16[512,6144]{1,0:T(8,128)(2,1)} %feat.1, bf16[384,512]{1,0:T(8,128)(2,1)} %head.1, s32[2]{0:T(128)} %seeds.1), custom_call_target="tpu_custom_call" | custom-call | flops 16106127360 | bytes 9000000 | tf_op jit(solution)/shard_map/pallas_call | solution.py:400
  89.6 2.6 %shard_map.51 = (f32[3072,128]{1,0:T(8,128)}, f32[2]{0:T(128)}) custom-call(bf16[2,8,3,64,128]{4,3,2,1,0:T(8,128)(2,1)} %get-tuple-element.6.sums, f32[8,128]{1,0:T(8,128)} %get-tuple-element.7.quot_in), custom_call_target="tpu_custom_call" | custom-call | tf_op jit(solution)/shard_map/pallas_call | solution.py:434
